TPU v7x, 32 devices: a whole 2x2x4 slice. The times are simulated.
32 devices in a mesh: segment: 4 (over y, x), tile: 8 (over z, core).
Axes of the slice: x: 2, y: 2, z: 4, core: 2. Of those that a mesh axis runs over, the one named last changes fastest.
Arguments:
- latent_clips: bfloat16 [4, 2, 32, 128, 128], P('segment', None, 'tile'), may hold values from -1.5 to 1.5
- augment_noise: bfloat16 [4, 4, 2, 32, 128, 128], P('segment', None, None, 'tile'), may hold values from -3.59375 to 3.59375
- section_weights: bfloat16 [4, 1152, 128], P('segment'), may hold values from -2 to 2
- frame_mixing: float32 [6, 128], replicated, may hold values from 0.1 to 0.9
- step_embed: float32 [6, 128], replicated, may hold values from -3 to 3
Outputs:
- sampled_clips: bfloat16 [4, 2, 32, 128, 128], P('segment', None, 'tile')
All inputs are finite; a program needn't handle non-finite values.
Results may differ from a plain program's by a relative error of at most 0.017.
Values may be sent and summed in bfloat16 or wider, within the bound.
No kernel may reach another device: no remote copies, remote signals or barrier semaphores. Data moves between devices by JAX's collectives and lax.ppermute only.
A program may use at most 64 MiB of HBM per device.

v0:
```python
import functools

import jax
import jax.numpy as jnp
from jax import lax
from jax.experimental import pallas as pl
from jax.experimental.pallas import tpu as pltpu
from jax.sharding import PartitionSpec as P

STEPS_BASE = 3
STEPS_SR = 1

norm_eps = 1e-06
keep_coef = 0.9
update_coef = 0.5
noise_coef = 0.5

HALO = 3
CHUNK = 64
SUBLANES = 8
f32 = jnp.float32
bf16 = jnp.bfloat16


def add_noise(latent, noise_piece):
    return (latent.astype(f32) + noise_coef * noise_piece.astype(f32)).astype(bf16)


def fill_taps(taps_ref, weight_ref, start):
    count, chans = weight_ref.shape
    row = taps_ref.shape[0] // 4
    weight = weight_ref[...]
    taps_ref[start : start + count, :chans] = weight
    taps_ref[row + start : row + start + count, chans:] = weight


def build_taps(taps_ref, core, place, mine_ref, other_ref):
    _, half, chans = mine_ref.shape
    row = taps_ref.shape[0] // 4
    taps_ref[3 * row :, :chans] = jnp.zeros((row, chans), bf16)
    taps_ref[:row, chans:] = jnp.zeros((row, chans), bf16)
    for flag, low, high in ((1 - core, mine_ref, other_ref), (core, other_ref, mine_ref)):

        @pl.when(flag == 1)
        def _(low=low, high=high):
            fill_taps(taps_ref, low.at[place], 0)
            fill_taps(taps_ref, high.at[place], half)


def taps_kernel(first, flags_ref, mine_ref, other_ref, taps_ref):
    for k in range(taps_ref.shape[0]):
        build_taps(taps_ref.at[k], 1 - flags_ref[2], flags_ref[3 + first + k], mine_ref, other_ref)


def make_taps(first, last, flags, mine, other):
    _, half, chans = mine.shape
    vmem = pl.BlockSpec(memory_space=pltpu.VMEM)
    return pl.pallas_call(
        functools.partial(taps_kernel, first),
        out_shape=jax.ShapeDtypeStruct((last - first, half // 3 * 8, 2 * chans), bf16),
        in_specs=[pl.BlockSpec(memory_space=pltpu.SMEM), vmem, vmem],
        out_specs=vmem,
        compiler_params=pltpu.CompilerParams(vmem_limit_bytes=16 * 1024 * 1024),
        cost_estimate=pl.CostEstimate(flops=0, bytes_accessed=(last - first) * half * 16 * chans, transcendentals=0),
    )(flags, mine, other)


def store_mixed(mixed_ref, state_ref, row, mixing, flag):
    frames, _, cols, chans = state_ref.shape
    first, second = [state_ref[frame, row] for frame in range(frames)]
    delta = (second - first) * mixing
    spot = lax.broadcasted_iota(jnp.int32, (SUBLANES, chans), 0)
    for index, mixed in enumerate((first + delta, second - delta)):
        if flag is not None:
            mixed = mixed * flag
        here = pl.ds(index * cols, cols)
        left, right = pltpu.roll(mixed, 1, 0), pltpu.roll(mixed, cols - 1, 0)
        left = jnp.concatenate([jnp.where(spot == 0, 0.0, left[:SUBLANES]), left[SUBLANES:]], axis=0)
        rest = cols - SUBLANES
        right = jnp.concatenate([right[:rest], jnp.where(spot == SUBLANES - 1, 0.0, right[rest:])], axis=0)
        mixed_ref[row, here, :chans] = left.astype(bf16)
        mixed_ref[row, here, chans : 2 * chans] = mixed.astype(bf16)
        mixed_ref[row, here, 2 * chans :] = right.astype(bf16)


def place_halos(even, buffer_ref, off_ref, on_ref, above, below):
    width = off_ref.shape[1]
    for flag, upper, lower in ((even, off_ref, on_ref), (1 - even, on_ref, off_ref)):

        @pl.when(flag == 1)
        def _(upper=upper, lower=lower):
            buffer_ref[:, above : above + width] = upper[...].astype(buffer_ref.dtype)
            buffer_ref[:, below : below + width] = lower[...].astype(buffer_ref.dtype)


def steps_kernel(
    first_step, sections, rows, noise_widths, sends, flags_ref, own_ref, first_ref, second_ref, per_step_ref, *rest
):
    total_rows = rows + 2 * HALO
    rest = list(rest)
    on_ref, off_ref = (first_ref, second_ref) if sends else (second_ref, first_ref)
    if sends:
        mine_ref, other_ref = rest.pop(0), rest.pop(0)
    else:
        taps_ref = rest.pop(0)
    noises = {k: rest.pop(0) for k, width in enumerate(noise_widths) if width is not None}
    wide = [k for k, width in enumerate(noise_widths) if width]
    if wide:
        noise_on_ref, noise_off_ref = rest.pop(0), rest.pop(0)
    out_ref = rest.pop(0)
    if sends:
        send_off_ref, send_on_ref = rest.pop(0), rest.pop(0)
    state_ref, mixed_ref, conv_ref = rest[:3]
    rest = rest[3:]
    if sends:
        taps_ref = rest.pop(0)
        build_taps(taps_ref.at[0], 1 - flags_ref[2], flags_ref[3], mine_ref, other_ref)
    else:
        rows_ref, sem = rest.pop(0), rest.pop(0)
    buffers = dict(zip(wide, rest))
    frames, _, cols, chans = own_ref.shape
    up_flag = flags_ref[0].astype(f32)
    down_flag = flags_ref[1].astype(f32)
    even = flags_ref[2]
    place_halos(even, state_ref, off_ref, on_ref, 0, HALO + rows)
    start = 0
    for step in wide:
        width = noise_widths[step]
        part = pl.ds(start, width)
        place_halos(
            even, buffers[step], noise_off_ref.at[:, part], noise_on_ref.at[:, part], HALO - width, HALO + rows
        )
        start += width
    def flag_of(row):
        if row < HALO:
            return up_flag
        if row >= HALO + rows:
            return down_flag
        return None

    def is_own(row):
        return HALO <= row < HALO + rows

    def mixing_of(step):
        return per_step_ref[first_step + step : first_step + step + 1, :]

    def first_mix(row):
        if is_own(row):
            for frame in range(frames):
                state_ref[frame, row] = own_ref[frame, row - HALO].astype(f32)
        store_mixed(mixed_ref.at[0], state_ref, row, mixing_of(0), flag_of(row))

    pixels = frames * cols

    def convolve(step, base, slot):
        source = mixed_ref.at[step % 2]
        taps = taps_ref.at[sections[step]]
        for frame in range(frames):
            here = pl.ds(frame * cols, cols)
            patches = jnp.concatenate([source[base + i, here] for i in range(4)], axis=1)
            conv_ref[pl.ds(slot * pixels + frame * cols, cols), :] = jnp.dot(
                patches, taps[...], preferred_element_type=f32
            )

    def update(step, base, slot):
        place = per_step_ref.shape[0] // 2 + first_step + step
        embed = per_step_ref[place : place + 1, :]
        last = step == HALO - 1
        for j in range(2):
            row = base + 1 + j
            for frame in range(frames):
                for spot in range(0, cols, CHUNK):
                    here = pl.ds(spot, CHUNK)
                    part = conv_ref[pl.ds(slot * pixels + frame * cols + spot, CHUNK), j * chans : (j + 1) * chans] + embed
                    mean = jnp.sum(part * part, axis=1, keepdims=True) * (4.0 / chans)
                    half = part * lax.rsqrt(mean + 4.0 * norm_eps)
                    silu = half + half * jnp.tanh(half)
                    new = keep_coef * state_ref[frame, row, here] + update_coef * silu
                    if step in noises:
                        if is_own(row):
                            piece = noises[step][frame, row - HALO, here]
                        else:
                            piece = buffers[step][frame, row, here]
                        new = new + noise_coef * piece.astype(f32)
                    if last:
                        (out_ref if sends else rows_ref)[frame, row - HALO, here] = new.astype(bf16)
                    else:
                        state_ref[frame, row, here] = new
            if last and not sends:
                copy_row(row - HALO).start()
            if not last:
                store_mixed(mixed_ref.at[(step + 1) % 2], state_ref, row, mixing_of(step + 1), flag_of(row))

    def copy_row(row):
        return pltpu.make_async_copy(rows_ref.at[:, row], out_ref.at[:, row], sem.at[row])

    waiting = None
    mixed_rows = 0
    slot = 0
    for step in range(HALO):
        for base in range(step, total_rows - step - 2, 2):
            if step == 0:
                while mixed_rows < base + 4:
                    first_mix(mixed_rows)
                    mixed_rows += 1
            convolve(step, base, slot)
            if waiting is not None:
                update(*waiting)
            waiting = (step, base, slot)
            slot = 1 - slot
    update(*waiting)
    if not sends:
        for row in range(rows):
            copy_row(row).wait()
    if sends:
        for flag, off_rows, on_rows in ((even, 0, rows - HALO), (1 - even, rows - HALO, 0)):

            @pl.when(flag == 1)
            def _(off_rows=off_rows, on_rows=on_rows):
                send_off_ref[...] = out_ref[:, off_rows : off_rows + HALO]
                send_on_ref[...] = out_ref[:, on_rows : on_rows + HALO]


def run_steps(first_step, sections, noise_widths, sends, flags, own, off, on, per_step, taps, noises):
    frames, rows, cols, chans = own.shape
    depth = 9 * chans
    total = rows + 2 * HALO
    vmem = pl.BlockSpec(memory_space=pltpu.VMEM)
    halos = (on, off) if sends else (off, on)
    operands = (flags, own, *halos, per_step, *taps, *noises)
    outputs = sum(total - 2 * (k + 1) for k in range(HALO)) * frames * cols
    state = pltpu.VMEM((frames, total, cols, chans), f32)
    edges = pltpu.VMEM((frames, total, cols, chans), bf16)
    edge = jax.ShapeDtypeStruct((frames, HALO, cols, chans), bf16)
    whole = jax.ShapeDtypeStruct(own.shape, bf16)
    return pl.pallas_call(
        functools.partial(steps_kernel, first_step, sections, rows, noise_widths, sends),
        out_shape=(whole, edge, edge) if sends else whole,
        in_specs=[pl.BlockSpec(memory_space=pltpu.SMEM)] + [vmem] * (len(operands) - 1),
        out_specs=(vmem, vmem, vmem) if sends else pl.BlockSpec(memory_space=pl.ANY),
        scratch_shapes=[
            state,
            pltpu.VMEM((2, total, frames * cols, 3 * chans), bf16),
            pltpu.VMEM((2 * frames * cols, 2 * chans), f32),
        ]
        + (
            [pltpu.VMEM((1, depth // 3 * 4, 2 * chans), bf16)]
            if sends
            else [pltpu.VMEM(own.shape, bf16), pltpu.SemaphoreType.DMA((rows,))]
        )
        + [edges for width in noise_widths if width],
        compiler_params=pltpu.CompilerParams(vmem_limit_bytes=40 * 1024 * 1024),
        cost_estimate=pl.CostEstimate(
            flops=2 * outputs * depth * chans, bytes_accessed=4 * own.size, transcendentals=outputs * chans
        ),
    )(*operands)


def off_swap(value):
    count = lax.axis_size("tile")
    return lax.ppermute(value, "tile", [p for i in range(1, count - 1, 2) for p in ((i, i + 1), (i + 1, i))])


def on_swap(value):
    return lax.ppermute(value, "tile", [(i, i ^ 1) for i in range(lax.axis_size("tile"))])


def edges_to_send(top, bottom):
    even = lax.axis_index("tile") % 2 == 0
    return jnp.where(even, top, bottom), jnp.where(even, bottom, top)


def per_device(latent_clips, augment_noise, section_weights, frame_mixing, step_embed):
    segment = lax.axis_index("segment")
    tile = lax.axis_index("tile")
    segments = lax.axis_size("segment")
    tiles = lax.axis_size("tile")
    weight = section_weights[0]
    half_rows = weight.shape[0] // 2

    def with_partner(value, d):
        return lax.ppermute(value, "segment", [(s, s ^ d) for s in range(segments)])

    def noise_for(clip):
        return lax.dynamic_index_in_dim(augment_noise[0], clip, 0, keepdims=False)

    order = [3, 1, 2]
    core = tile % 2

    noises = {d: with_partner(noise_for(segment ^ d), d) for d in order}

    weight, noises[order[1]] = lax.optimization_barrier((weight, noises[order[1]]))
    half = lax.dynamic_slice_in_dim(weight, core * half_rows, half_rows, 0)
    halves = {d: with_partner(half, d) for d in order}
    halves[0] = half
    mine = jnp.stack([halves[d] for d in reversed(range(segments))])
    other = on_swap(mine)

    per_step = jnp.concatenate([0.5 * frame_mixing, step_embed])
    flags = jnp.stack(
        [(tile > 0).astype(jnp.int32), (tile < tiles - 1).astype(jnp.int32), 1 - core]
        + [segments - 1 - (segment ^ s) for s in range(segments)]
    )
    start = latent_clips[0].astype(f32)
    noises[order[2]], noises[0], start, per_step, flags = lax.optimization_barrier(
        (noises[order[2]], noise_for(segment), start, per_step, flags)
    )

    def noise_of(section):
        return lax.select_n(segment ^ section, *[noises[d] for d in range(segments)])

    latent = add_noise(start, noise_of(0))
    rows = latent.shape[1]
    late = [noise_of(2), noise_of(3)]
    noise_edges = [
        jnp.concatenate([late[0][:, :2], late[1][:, :1]], axis=1),
        jnp.concatenate([late[0][:, rows - 2 :], late[1][:, rows - 1 :]], axis=1),
    ]
    off_send, on_send = edges_to_send(latent[:, :HALO], latent[:, rows - HALO :])
    off_noise, on_noise = edges_to_send(*noise_edges)
    on, off = on_swap(on_send), off_swap(off_send)
    noise_on, noise_off = on_swap(on_noise), off_swap(off_noise)

    latent, send_off, send_on = run_steps(
        0, (0,) * STEPS_BASE, (None, None, 0), True, flags, latent, off, on, per_step, (mine, other), (noise_of(1),)
    )
    mine, other, latent = lax.optimization_barrier((mine, other, latent))
    off = off_swap(send_off)
    on = on_swap(send_on)
    taps = make_taps(1, segments, flags, mine, other)
    latent = run_steps(
        STEPS_BASE,
        (0, 1, 2),
        (2, 1, None),
        False,
        flags,
        latent,
        off,
        on,
        per_step,
        (taps,),
        (late[0], late[1], noise_on, noise_off),
    )
    return latent[None]


def solution(mesh):
    return jax.shard_map(
        per_device,
        mesh=mesh,
        in_specs=(
            P("segment", None, "tile", None, None),
            P("segment", None, None, "tile", None, None),
            P("segment", None, None),
            P(),
            P(),
        ),
        out_specs=P("segment", None, "tile", None, None),
        check_vma=False,
    )
```

profile of v0, /device:TPU:1, one launch (start us, length us, event | category | flops | bytes accessed | tf_op | source)
XLA Modules:
  0.0 43.0 jit_solution(11140004616968010887)
XLA Ops:
  0.0 0.0 copy-start
  0.0 0.0 copy-start.1
  0.0 0.0 copy-start.2
  0.0 1.3 %dynamic-slice_bitcast_fusion = (bf16[2,4,128,128]{3,2,1,0:T(8,128)(2,1)S(1)}, bf16[2,4,128,128]{3,2,1,0:T(8,128)(2,1)S(1)}, bf16[2,4,128,128]{3,2,1,0:T(8,128)(2,1)S(1)}, bf16[2,4,128,128]{3,2,1,0:T(8,128)(2,1)S(1)}) fusion(bf16[1,4,2,4,128,128]{5,4,3,2,1,0:T(8,128)(2,1)} %param.6, s32[]{:T(128)S(6)} %select_n.167, s32[]{:T(128)S(6)} %select_n.156, ...), kind=kLoop, calls=%fused_computation.6 | loop fusion | bytes 2097168 | tf_op jit(solution)/shard_map/jit(dynamic_index_in_dim)/squeeze | solution.py:285
  1.3 2.1 %collective-permute-start = (bf16[2,4,128,128]{3,2,1,0:T(8,128)(2,1)S(1)}, bf16[2,4,128,128]{3,2,1,0:T(8,128)(2,1)S(1)}, u32[]{:S(2)}, u32[]{:S(2)}) collective-permute-start(bf16[2,4,128,128]{3,2,1,0:T(8,128)(2,1)S(1)} %get-tuple-element.36), channel_id=1, source_target_pairs={{0,16},{8,24},{16,0},{24,8},{1,17},{9,25},{17,1},{25,9},{2,18},{10... | collective-permute-start | bytes 786440 | tf_op jit(solution)/shard_map/ppermute | solution.py:282
  3.5 1.2 %collective-permute-start.1 = (bf16[2,4,128,128]{3,2,1,0:T(8,128)(2,1)S(1)}, bf16[2,4,128,128]{3,2,1,0:T(8,128)(2,1)S(1)}, u32[]{:S(2)}, u32[]{:S(2)}) collective-permute-start(bf16[2,4,128,128]{3,2,1,0:T(8,128)(2,1)S(1)} %get-tuple-element.37), channel_id=1, source_target_pairs={{0,8},{8,0},{16,24},{24,16},{1,9},{9,1},{17,25},{25,17},{2,10},{10... | collective-permute-start | bytes 786440 | tf_op jit(solution)/shard_map/ppermute | solution.py:282
  4.7 0.0 collective-permute-start.6
  4.7 1.0 %bitcast_convert_fusion = f32[2,4,128,128]{3,2,1,0:T(8,128)S(1)} fusion(bf16[1,2,4,128,128]{4,3,2,1,0:T(8,128)(2,1)} %param.5), kind=kLoop, calls=%fused_computation.2 | loop fusion | flops 131072 | bytes 786432 | tf_op jit(solution)/shard_map/convert_element_type | solution.py:304
  5.7 0.0 copy-done.1
  5.8 0.1 stack.54.flags_ref
  5.9 0.0 copy-done.2
  5.9 4.4 %collective-permute-done.1 = bf16[2,4,128,128]{3,2,1,0:T(8,128)(2,1)S(1)} collective-permute-done((bf16[2,4,128,128]{3,2,1,0:T(8,128)(2,1)S(1)}, bf16[2,4,128,128]{3,2,1,0:T(8,128)(2,1)S(1)}, u32[]{:S(2)}, u32[]{:S(2)}) %collective-permute-start.1) | collective-permute-done | bytes 262176 | tf_op jit(solution)/shard_map/ppermute | solution.py:282
  10.3 0.0 copy-done
  10.3 1.3 %collective-permute-start.4 = (bf16[576,128]{1,0:T(8,128)(2,1)S(1)}, bf16[576,128]{1,0:T(8,128)(2,1)S(1)}, u32[]{:S(2)}, u32[]{:S(2)}) collective-permute-start(bf16[576,128]{1,0:T(8,128)(2,1)S(1)} %constant_dynamic-slice_fusion), channel_id=1, source_target_pairs={{0,8},{8,0},{16,24},{24,16},{1,9},{9,1},{17,25},{25,17},{2,10},{10... | collective-permute-start | bytes 442376 | tf_op jit(solution)/shard_map/ppermute | solution.py:282
  11.6 0.2 collective-permute-start.3
  11.9 1.2 %collective-permute-start.2 = (bf16[576,128]{1,0:T(8,128)(2,1)S(1)}, bf16[576,128]{1,0:T(8,128)(2,1)S(1)}, u32[]{:S(2)}, u32[]{:S(2)}) collective-permute-start(bf16[576,128]{1,0:T(8,128)(2,1)S(1)} %constant_dynamic-slice_fusion), channel_id=1, source_target_pairs={{0,24},{8,16},{16,8},{24,0},{1,25},{9,17},{17,9},{25,1},{2,26},{10... | collective-permute-start | bytes 442376 | tf_op jit(solution)/shard_map/ppermute | solution.py:282
  13.1 0.0 collective-permute-done
  13.1 3.0 %collective-permute-done.6 = bf16[2,4,128,128]{3,2,1,0:T(8,128)(2,1)S(1)} collective-permute-done((bf16[2,4,128,128]{3,2,1,0:T(8,128)(2,1)S(1)}, bf16[2,4,128,128]{3,2,1,0:T(8,128)(2,1)S(1)}, u32[]{:S(2)}, u32[]{:S(2)}) %collective-permute-start.6) | collective-permute-done | bytes 262176 | tf_op jit(solution)/shard_map/ppermute | solution.py:282
  16.1 0.2 add_convert_fusion.own_ref
  16.3 2.8 %collective-permute-start.7 = (bf16[2,3,128,128]{3,2,1,0:T(8,128)(2,1)S(1)}, bf16[2,3,128,128]{3,2,1,0:T(8,128)(2,1)S(1)}, u32[]{:S(2)}, u32[]{:S(2)}) collective-permute-start(bf16[2,3,128,128]{3,2,1,0:T(8,128)(2,1)S(1)} %get-tuple-element.45), channel_id=1, source_target_pairs={{0,1},{1,0},{2,3},{3,2},{4,5},{5,4},{6,7},{7,6},{8,9},{9,8},{10,11... | collective-permute-start | bytes 589832 | tf_op jit(solution)/shard_map/ppermute | solution.py:265
  19.1 3.6 %collective-permute-start.8 = (bf16[2,3,128,128]{3,2,1,0:T(8,128)(2,1)S(1)}, bf16[2,3,128,128]{3,2,1,0:T(8,128)(2,1)S(1)}, u32[]{:S(2)}, u32[]{:S(2)}) collective-permute-start(bf16[2,3,128,128]{3,2,1,0:T(8,128)(2,1)S(1)} %get-tuple-element.44), channel_id=1, source_target_pairs={{1,2},{2,1},{3,4},{4,3},{5,6},{6,5},{9,10},{10,9},{11,12},{12,11},... | collective-permute-start | bytes 589832 | tf_op jit(solution)/shard_map/ppermute | solution.py:261
  22.7 0.0 collective-permute-done.4
  22.7 0.0 collective-permute-done.3
  22.7 0.0 collective-permute-done.2
  22.7 0.1 pad_maximum_fusion.rest_0_.mine_ref
  22.8 1.3 %collective-permute-start.5 = (bf16[4,576,128]{2,1,0:T(8,128)(2,1)S(1)}, bf16[4,576,128]{2,1,0:T(8,128)(2,1)S(1)}, u32[]{:S(2)}, u32[]{:S(2)}) collective-permute-start(bf16[4,576,128]{2,1,0:T(8,128)(2,1)S(1)} %pad_maximum_fusion.rest_0_.mine_ref), channel_id=1, source_target_pairs={{0,1},{1,0},{2,3},{3,2},{4,5},{5,4},{6,7},{7,6},{8,9},{9,8},{10,11... | collective-permute-start | bytes 1769480 | tf_op jit(solution)/shard_map/ppermute | solution.py:265
  24.1 0.1 select_select_fusion
  24.3 0.1 collective-permute-start.11
  24.4 3.7 %collective-permute-start.12 = (bf16[2,3,128,128]{3,2,1,0:T(8,128)(2,1)S(1)}, bf16[2,3,128,128]{3,2,1,0:T(8,128)(2,1)S(1)}, u32[]{:S(2)}, u32[]{:S(2)}) collective-permute-start(bf16[2,3,128,128]{3,2,1,0:T(8,128)(2,1)S(1)} %get-tuple-element.38), channel_id=1, source_target_pairs={{1,2},{2,1},{3,4},{4,3},{5,6},{6,5},{9,10},{10,9},{11,12},{12,11},... | collective-permute-start | bytes 589832 | tf_op jit(solution)/shard_map/ppermute | solution.py:261
  28.1 0.0 collective-permute-done.7.first_ref
  28.1 0.0 collective-permute-done.8.second_ref
  28.1 0.0 collective-permute-done.5.rest_1_.other_ref
  28.1 3.4 %shard_map.55 = (bf16[2,4,128,128]{3,2,1,0:T(8,128)(2,1)S(1)}, bf16[2,3,128,128]{3,2,1,0:T(8,128)(2,1)S(1)}, bf16[2,3,128,128]{3,2,1,0:T(8,128)(2,1)S(1)}) custom-call(s32[7]{0:T(128)S(1)} %stack.54.flags_ref, bf16[2,4,128,128]{3,2,1,0:T(8,128)(2,1)S(1)} %add_convert_fusion.own_ref, bf16[2,3,128,128]{3,2,1,0:T(8,128)(2,1)S(1)} %collective-permute-done.7.first_ref, ...), custom_call_target="tpu_custom_call" | custom-call | flops 1358954496 | bytes 524288 | tf_op jit(solution)/shard_map/pallas_call | solution.py:236
  31.6 1.9 %collective-permute-start.9 = (bf16[2,3,128,128]{3,2,1,0:T(8,128)(2,1)S(1)}, bf16[2,3,128,128]{3,2,1,0:T(8,128)(2,1)S(1)}, u32[]{:S(2)}, u32[]{:S(2)}) collective-permute-start(bf16[2,3,128,128]{3,2,1,0:T(8,128)(2,1)S(1)} %get-tuple-element.27), channel_id=1, source_target_pairs={{1,2},{2,1},{3,4},{4,3},{5,6},{6,5},{9,10},{10,9},{11,12},{12,11},... | collective-permute-start | bytes 589832 | tf_op jit(solution)/shard_map/ppermute | solution.py:261
  33.5 0.1 collective-permute-start.10
  33.6 0.9 %shard_map.56.rest_0_ = bf16[3,1536,256]{2,1,0:T(8,128)(2,1)S(1)} custom-call(s32[7]{0:T(128)S(1)} %stack.54.flags_ref, bf16[4,576,128]{2,1,0:T(8,128)(2,1)S(1)} %pad_maximum_fusion.rest_0_.mine_ref, bf16[4,576,128]{2,1,0:T(8,128)(2,1)S(1)} %collective-permute-done.5.rest_1_.other_ref), custom_call_target="tpu_custom_call" | custom-call | bytes 3538944 | tf_op jit(solution)/shard_map/pallas_call | solution.py:58
  34.4 0.0 collective-permute-done.11.rest_3_
  34.4 0.0 collective-permute-done.12.rest_4_
  34.4 4.1 %collective-permute-done.9.first_ref = bf16[2,3,128,128]{3,2,1,0:T(8,128)(2,1)S(1)} collective-permute-done((bf16[2,3,128,128]{3,2,1,0:T(8,128)(2,1)S(1)}, bf16[2,3,128,128]{3,2,1,0:T(8,128)(2,1)S(1)}, u32[]{:S(2)}, u32[]{:S(2)}) %collective-permute-start.9) | collective-permute-done | bytes 196640 | tf_op jit(solution)/shard_map/ppermute | solution.py:261
  38.5 0.0 collective-permute-done.10.second_ref
  38.5 4.5 %shard_map.57 = bf16[2,4,128,128]{3,2,1,0:T(8,128)(2,1)} custom-call(s32[7]{0:T(128)S(1)} %stack.54.flags_ref, bf16[2,4,128,128]{3,2,1,0:T(8,128)(2,1)S(1)} %get-tuple-element.26.own_ref, bf16[2,3,128,128]{3,2,1,0:T(8,128)(2,1)S(1)} %collective-permute-done.9.first_ref, bf16[2,3,128,128]{3,2,1,0:T(8,128)(2,1)S(1)} %collective-permute-done.10.second_ref, ...), custom_call_target="tpu_custom_call" | custom-call | flops 1358954496 | bytes 524288 | tf_op jit(solution)/shard_map/pallas_call | solution.py:236
  (8 shorter events, 0.1 us)
Async XLA Ops:
  0.0 10.3 %copy-start = (bf16[1,1152,128]{2,1,0:T(8,128)(2,1)S(1)}, bf16[1,1152,128]{2,1,0:T(8,128)(2,1)}, u32[]{:S(2)}) copy-start(bf16[1,1152,128]{2,1,0:T(8,128)(2,1)} %param.7) | copy-start | bytes 884740
  0.0 5.7 %copy-start.1 = (f32[6,128]{1,0:T(8,128)S(1)}, f32[6,128]{1,0:T(8,128)}, u32[]{:S(2)}) copy-start(f32[6,128]{1,0:T(8,128)} %param.8) | copy-start | bytes 9220
  0.0 5.9 %copy-start.2 = (f32[6,128]{1,0:T(8,128)S(1)}, f32[6,128]{1,0:T(8,128)}, u32[]{:S(2)}) copy-start(f32[6,128]{1,0:T(8,128)} %param.9) | copy-start | bytes 9220
  1.3 11.7 %collective-permute-start = (bf16[2,4,128,128]{3,2,1,0:T(8,128)(2,1)S(1)}, bf16[2,4,128,128]{3,2,1,0:T(8,128)(2,1)S(1)}, u32[]{:S(2)}, u32[]{:S(2)}) collective-permute-start(bf16[2,4,128,128]{3,2,1,0:T(8,128)(2,1)S(1)} %get-tuple-element.36), channel_id=1, source_target_pairs={{0,16},{8,24},{16,0},{24,8},{1,17},{9,25},{17,1},{25,9},{2,18},{10... | collective-permute-start | bytes 786440 | tf_op jit(solution)/shard_map/ppermute | solution.py:282
  3.5 6.9 %collective-permute-start.1 = (bf16[2,4,128,128]{3,2,1,0:T(8,128)(2,1)S(1)}, bf16[2,4,128,128]{3,2,1,0:T(8,128)(2,1)S(1)}, u32[]{:S(2)}, u32[]{:S(2)}) collective-permute-start(bf16[2,4,128,128]{3,2,1,0:T(8,128)(2,1)S(1)} %get-tuple-element.37), channel_id=1, source_target_pairs={{0,8},{8,0},{16,24},{24,16},{1,9},{9,1},{17,25},{25,17},{2,10},{10... | collective-permute-start | bytes 786440 | tf_op jit(solution)/shard_map/ppermute | solution.py:282
  4.7 11.4 %collective-permute-start.6 = (bf16[2,4,128,128]{3,2,1,0:T(8,128)(2,1)S(1)}, bf16[2,4,128,128]{3,2,1,0:T(8,128)(2,1)S(1)}, u32[]{:S(2)}, u32[]{:S(2)}) collective-permute-start(bf16[2,4,128,128]{3,2,1,0:T(8,128)(2,1)S(1)} %get-tuple-element.34), channel_id=1, source_target_pairs={{0,24},{8,16},{16,8},{24,0},{1,25},{9,17},{17,9},{25,1},{2,26},{10... | collective-permute-start | bytes 786440 | tf_op jit(solution)/shard_map/ppermute | solution.py:282
  10.3 12.3 %collective-permute-start.4 = (bf16[576,128]{1,0:T(8,128)(2,1)S(1)}, bf16[576,128]{1,0:T(8,128)(2,1)S(1)}, u32[]{:S(2)}, u32[]{:S(2)}) collective-permute-start(bf16[576,128]{1,0:T(8,128)(2,1)S(1)} %constant_dynamic-slice_fusion), channel_id=1, source_target_pairs={{0,8},{8,0},{16,24},{24,16},{1,9},{9,1},{17,25},{25,17},{2,10},{10... | collective-permute-start | bytes 442376 | tf_op jit(solution)/shard_map/ppermute | solution.py:282
  11.6 11.0 %collective-permute-start.3 = (bf16[576,128]{1,0:T(8,128)(2,1)S(1)}, bf16[576,128]{1,0:T(8,128)(2,1)S(1)}, u32[]{:S(2)}, u32[]{:S(2)}) collective-permute-start(bf16[576,128]{1,0:T(8,128)(2,1)S(1)} %constant_dynamic-slice_fusion), channel_id=1, source_target_pairs={{0,16},{8,24},{16,0},{24,8},{1,17},{9,25},{17,1},{25,9},{2,18},{10... | collective-permute-start | bytes 442376 | tf_op jit(solution)/shard_map/ppermute | solution.py:282
  11.9 10.8 %collective-permute-start.2 = (bf16[576,128]{1,0:T(8,128)(2,1)S(1)}, bf16[576,128]{1,0:T(8,128)(2,1)S(1)}, u32[]{:S(2)}, u32[]{:S(2)}) collective-permute-start(bf16[576,128]{1,0:T(8,128)(2,1)S(1)} %constant_dynamic-slice_fusion), channel_id=1, source_target_pairs={{0,24},{8,16},{16,8},{24,0},{1,25},{9,17},{17,9},{25,1},{2,26},{10... | collective-permute-start | bytes 442376 | tf_op jit(solution)/shard_map/ppermute | solution.py:282
  16.3 11.8 %collective-permute-start.7 = (bf16[2,3,128,128]{3,2,1,0:T(8,128)(2,1)S(1)}, bf16[2,3,128,128]{3,2,1,0:T(8,128)(2,1)S(1)}, u32[]{:S(2)}, u32[]{:S(2)}) collective-permute-start(bf16[2,3,128,128]{3,2,1,0:T(8,128)(2,1)S(1)} %get-tuple-element.45), channel_id=1, source_target_pairs={{0,1},{1,0},{2,3},{3,2},{4,5},{5,4},{6,7},{7,6},{8,9},{9,8},{10,11... | collective-permute-start | bytes 589832 | tf_op jit(solution)/shard_map/ppermute | solution.py:265
  19.1 9.0 %collective-permute-start.8 = (bf16[2,3,128,128]{3,2,1,0:T(8,128)(2,1)S(1)}, bf16[2,3,128,128]{3,2,1,0:T(8,128)(2,1)S(1)}, u32[]{:S(2)}, u32[]{:S(2)}) collective-permute-start(bf16[2,3,128,128]{3,2,1,0:T(8,128)(2,1)S(1)} %get-tuple-element.44), channel_id=1, source_target_pairs={{1,2},{2,1},{3,4},{4,3},{5,6},{6,5},{9,10},{10,9},{11,12},{12,11},... | collective-permute-start | bytes 589832 | tf_op jit(solution)/shard_map/ppermute | solution.py:261
  22.8 5.3 %collective-permute-start.5 = (bf16[4,576,128]{2,1,0:T(8,128)(2,1)S(1)}, bf16[4,576,128]{2,1,0:T(8,128)(2,1)S(1)}, u32[]{:S(2)}, u32[]{:S(2)}) collective-permute-start(bf16[4,576,128]{2,1,0:T(8,128)(2,1)S(1)} %pad_maximum_fusion.rest_0_.mine_ref), channel_id=1, source_target_pairs={{0,1},{1,0},{2,3},{3,2},{4,5},{5,4},{6,7},{7,6},{8,9},{9,8},{10,11... | collective-permute-start | bytes 1769480 | tf_op jit(solution)/shard_map/ppermute | solution.py:265
  24.3 10.1 %collective-permute-start.11 = (bf16[2,3,128,128]{3,2,1,0:T(8,128)(2,1)S(1)}, bf16[2,3,128,128]{3,2,1,0:T(8,128)(2,1)S(1)}, u32[]{:S(2)}, u32[]{:S(2)}) collective-permute-start(bf16[2,3,128,128]{3,2,1,0:T(8,128)(2,1)S(1)} %get-tuple-element.39), channel_id=1, source_target_pairs={{0,1},{1,0},{2,3},{3,2},{4,5},{5,4},{6,7},{7,6},{8,9},{9,8},{10,11... | collective-permute-start | bytes 589832 | tf_op jit(solution)/shard_map/ppermute | solution.py:265
  24.4 10.1 %collective-permute-start.12 = (bf16[2,3,128,128]{3,2,1,0:T(8,128)(2,1)S(1)}, bf16[2,3,128,128]{3,2,1,0:T(8,128)(2,1)S(1)}, u32[]{:S(2)}, u32[]{:S(2)}) collective-permute-start(bf16[2,3,128,128]{3,2,1,0:T(8,128)(2,1)S(1)} %get-tuple-element.38), channel_id=1, source_target_pairs={{1,2},{2,1},{3,4},{4,3},{5,6},{6,5},{9,10},{10,9},{11,12},{12,11},... | collective-permute-start | bytes 589832 | tf_op jit(solution)/shard_map/ppermute | solution.py:261
  31.6 7.0 %collective-permute-start.9 = (bf16[2,3,128,128]{3,2,1,0:T(8,128)(2,1)S(1)}, bf16[2,3,128,128]{3,2,1,0:T(8,128)(2,1)S(1)}, u32[]{:S(2)}, u32[]{:S(2)}) collective-permute-start(bf16[2,3,128,128]{3,2,1,0:T(8,128)(2,1)S(1)} %get-tuple-element.27), channel_id=1, source_target_pairs={{1,2},{2,1},{3,4},{4,3},{5,6},{6,5},{9,10},{10,9},{11,12},{12,11},... | collective-permute-start | bytes 589832 | tf_op jit(solution)/shard_map/ppermute | solution.py:261
  33.5 5.1 %collective-permute-start.10 = (bf16[2,3,128,128]{3,2,1,0:T(8,128)(2,1)S(1)}, bf16[2,3,128,128]{3,2,1,0:T(8,128)(2,1)S(1)}, u32[]{:S(2)}, u32[]{:S(2)}) collective-permute-start(bf16[2,3,128,128]{3,2,1,0:T(8,128)(2,1)S(1)} %get-tuple-element.28), channel_id=1, source_target_pairs={{0,1},{1,0},{2,3},{3,2},{4,5},{5,4},{6,7},{7,6},{8,9},{9,8},{10,11... | collective-permute-start | bytes 589832 | tf_op jit(solution)/shard_map/ppermute | solution.py:265
where the time goes:
time: 43.2 us; the launch traced here: 43 us
  starting transfers between devices  19.5 us (45%)
  waiting for transfers between devices  11.6 us (27%)
  Pallas kernels  8.75 us (20%)
  local copies, waits for them, and re-layouts  1.46 us (3%)
  other arithmetic  1.42 us (3%)
    ppermute x3, starting transfers between devices, off_swap(): lax.ppermute(value, 'tile', [p for i in range(1, count - 1, 2) for p in (...  9.17 us
    pallas_call x2, Pallas kernels, run_steps(): pl.pallas_call(functools.partial(steps_kernel, first_step, sections, rows...  7.89 us
    ppermute x6, waiting for transfers between devices, with_partner(): return lax.ppermute(value, 'segment', [(s, s ^ d) for s in range(segments)])  7.45 us
    ppermute x6, starting transfers between devices, with_partner(): return lax.ppermute(value, 'segment', [(s, s ^ d) for s in range(segments)])  6.11 us
    ppermute x4, starting transfers between devices, on_swap(): lax.ppermute(value, 'tile', [(i, i ^ 1) for i in range(lax.axis_size('til...  4.24 us
    ppermute x3, waiting for transfers between devices, off_swap(): lax.ppermute(value, 'tile', [p for i in range(1, count - 1, 2) for p in (...  4.1 us
    squeeze x1, local copies, waits for them, and re-layouts, noise_for(): return lax.dynamic_index_in_dim(augment_noise[0], clip, 0, keepdims=False)  1.3 us
    convert_element_type x1, other arithmetic, per_device(): start = latent_clips[0].astype(f32)  0.98 us
  transfers between devices with their start and end apart: 13, of which 3 were waited for; matrix products, arithmetic and copies ran while one was open for 4% of the time, Pallas kernels for 10%

commit v1 on v0

--- a/solution.py
+++ b/solution.py
@@ -47,22 +47,27 @@
             fill_taps(taps_ref, high.at[place], half)
 
 
-def taps_kernel(first, flags_ref, mine_ref, other_ref, taps_ref):
+def half_place(section):
+    return lax.axis_size("segment") - 1 - (lax.axis_index("segment") ^ section)
+
+
+def taps_kernel(first, mine_ref, other_ref, taps_ref):
+    core = lax.axis_index("tile") % 2
     for k in range(taps_ref.shape[0]):
-        build_taps(taps_ref.at[k], 1 - flags_ref[2], flags_ref[3 + first + k], mine_ref, other_ref)
-
-
-def make_taps(first, last, flags, mine, other):
+        build_taps(taps_ref.at[k], core, half_place(first + k), mine_ref, other_ref)
+
+
+def make_taps(first, last, mine, other):
     _, half, chans = mine.shape
     vmem = pl.BlockSpec(memory_space=pltpu.VMEM)
     return pl.pallas_call(
         functools.partial(taps_kernel, first),
         out_shape=jax.ShapeDtypeStruct((last - first, half // 3 * 8, 2 * chans), bf16),
-        in_specs=[pl.BlockSpec(memory_space=pltpu.SMEM), vmem, vmem],
+        in_specs=[vmem, vmem],
         out_specs=vmem,
         compiler_params=pltpu.CompilerParams(vmem_limit_bytes=16 * 1024 * 1024),
         cost_estimate=pl.CostEstimate(flops=0, bytes_accessed=(last - first) * half * 16 * chans, transcendentals=0),
-    )(flags, mine, other)
+    )(mine, other)
 
 
 def store_mixed(mixed_ref, state_ref, row, mixing, flag):
@@ -94,10 +99,11 @@
 
 
 def steps_kernel(
-    first_step, sections, rows, noise_widths, sends, flags_ref, own_ref, first_ref, second_ref, per_step_ref, *rest
+    first_step, sections, rows, noise_widths, sends, own_ref, first_ref, second_ref, per_step_ref, *rest
 ):
     total_rows = rows + 2 * HALO
     rest = list(rest)
+    tile = lax.axis_index("tile")
     on_ref, off_ref = (first_ref, second_ref) if sends else (second_ref, first_ref)
     if sends:
         mine_ref, other_ref = rest.pop(0), rest.pop(0)
@@ -106,7 +112,7 @@
     noises = {k: rest.pop(0) for k, width in enumerate(noise_widths) if width is not None}
     wide = [k for k, width in enumerate(noise_widths) if width]
     if wide:
-        noise_on_ref, noise_off_ref = rest.pop(0), rest.pop(0)
+        noise_off_ref, noise_on_ref = rest.pop(0), rest.pop(0)
     out_ref = rest.pop(0)
     if sends:
         send_off_ref, send_on_ref = rest.pop(0), rest.pop(0)
@@ -114,14 +120,14 @@
     rest = rest[3:]
     if sends:
         taps_ref = rest.pop(0)
-        build_taps(taps_ref.at[0], 1 - flags_ref[2], flags_ref[3], mine_ref, other_ref)
+        build_taps(taps_ref.at[0], tile % 2, half_place(0), mine_ref, other_ref)
     else:
         rows_ref, sem = rest.pop(0), rest.pop(0)
     buffers = dict(zip(wide, rest))
     frames, _, cols, chans = own_ref.shape
-    up_flag = flags_ref[0].astype(f32)
-    down_flag = flags_ref[1].astype(f32)
-    even = flags_ref[2]
+    up_flag = jnp.where(tile > 0, 1.0, 0.0)
+    down_flag = jnp.where(tile < lax.axis_size("tile") - 1, 1.0, 0.0)
+    even = 1 - tile % 2
     place_halos(even, state_ref, off_ref, on_ref, 0, HALO + rows)
     start = 0
     for step in wide:
@@ -221,13 +227,13 @@
                 send_on_ref[...] = out_ref[:, on_rows : on_rows + HALO]
 
 
-def run_steps(first_step, sections, noise_widths, sends, flags, own, off, on, per_step, taps, noises):
+def run_steps(first_step, sections, noise_widths, sends, own, off, on, per_step, taps, noises):
     frames, rows, cols, chans = own.shape
     depth = 9 * chans
     total = rows + 2 * HALO
     vmem = pl.BlockSpec(memory_space=pltpu.VMEM)
     halos = (on, off) if sends else (off, on)
-    operands = (flags, own, *halos, per_step, *taps, *noises)
+    operands = (own, *halos, per_step, *taps, *noises)
     outputs = sum(total - 2 * (k + 1) for k in range(HALO)) * frames * cols
     state = pltpu.VMEM((frames, total, cols, chans), f32)
     edges = pltpu.VMEM((frames, total, cols, chans), bf16)
@@ -236,7 +242,7 @@
     return pl.pallas_call(
         functools.partial(steps_kernel, first_step, sections, rows, noise_widths, sends),
         out_shape=(whole, edge, edge) if sends else whole,
-        in_specs=[pl.BlockSpec(memory_space=pltpu.SMEM)] + [vmem] * (len(operands) - 1),
+        in_specs=[vmem] * len(operands),
         out_specs=(vmem, vmem, vmem) if sends else pl.BlockSpec(memory_space=pl.ANY),
         scratch_shapes=[
             state,
@@ -297,13 +303,9 @@
     other = on_swap(mine)
 
     per_step = jnp.concatenate([0.5 * frame_mixing, step_embed])
-    flags = jnp.stack(
-        [(tile > 0).astype(jnp.int32), (tile < tiles - 1).astype(jnp.int32), 1 - core]
-        + [segments - 1 - (segment ^ s) for s in range(segments)]
-    )
     start = latent_clips[0].astype(f32)
-    noises[order[2]], noises[0], start, per_step, flags = lax.optimization_barrier(
-        (noises[order[2]], noise_for(segment), start, per_step, flags)
+    noises[order[2]], noises[0], start, per_step = lax.optimization_barrier(
+        (noises[order[2]], noise_for(segment), start, per_step)
     )
 
     def noise_of(section):
@@ -322,24 +324,23 @@
     noise_on, noise_off = on_swap(on_noise), off_swap(off_noise)
 
     latent, send_off, send_on = run_steps(
-        0, (0,) * STEPS_BASE, (None, None, 0), True, flags, latent, off, on, per_step, (mine, other), (noise_of(1),)
+        0, (0,) * STEPS_BASE, (None, None, 0), True, latent, off, on, per_step, (mine, other), (noise_of(1),)
     )
     mine, other, latent = lax.optimization_barrier((mine, other, latent))
     off = off_swap(send_off)
     on = on_swap(send_on)
-    taps = make_taps(1, segments, flags, mine, other)
+    taps = make_taps(1, segments, mine, other)
     latent = run_steps(
         STEPS_BASE,
         (0, 1, 2),
         (2, 1, None),
         False,
-        flags,
         latent,
         off,
         on,
         per_step,
         (taps,),
-        (late[0], late[1], noise_on, noise_off),
+        (late[0], late[1], noise_off, noise_on),
     )
     return latent[None]
 

time: 43.2 us -> 41.8 us (0.968)
  Pallas kernels: 8.75 us -> 7.23 us
  starting transfers between devices: 19.5 us -> 20.6 us
  waiting for transfers between devices: 11.6 us -> 10.7 us
    ppermute x3, waiting for transfers between devices: 4.1 us -> 3 us  [off_swap(): lax.ppermute(value, 'tile', [p for i in range(1, count - 1, 2) for p in (...]
    pallas_call x2, Pallas kernels: 7.89 us -> 6.91 us  [run_steps(): pl.pallas_call(functools.partial(steps_kernel, first_step, sections, rows...]
    ppermute x3, starting transfers between devices: 9.17 us -> 9.78 us  [off_swap(): lax.ppermute(value, 'tile', [p for i in range(1, count - 1, 2) for p in (...]
    pallas_call x1, Pallas kernels: 0.86 us -> 0.31 us  [make_taps(): pl.pallas_call(functools.partial(taps_kernel, first), out_shape=jax.Shape...]
    ppermute x4, starting transfers between devices: 4.24 us -> 4.73 us  [on_swap(): lax.ppermute(value, 'tile', [(i, i ^ 1) for i in range(lax.axis_size('til...]
  transfers between devices with their start and end apart: 13 -> 13, of which waited for: 3 -> 4; matrix products, arithmetic and copies ran while one was open for 4% -> 4% of each run, Pallas kernels for 10% -> 8%
where the time goes in v1:
time: 41.8 us; the launch traced here: 41.6 us
  starting transfers between devices  20.6 us (49%)
  waiting for transfers between devices  10.7 us (26%)
  Pallas kernels  7.23 us (17%)
  other arithmetic  1.42 us (3%)
  local copies, waits for them, and re-layouts  1.37 us (3%)
    ppermute x3, starting transfers between devices, off_swap(): lax.ppermute(value, 'tile', [p for i in range(1, count - 1, 2) for p in (...  9.78 us
    ppermute x6, waiting for transfers between devices, with_partner(): return lax.ppermute(value, 'segment', [(s, s ^ d) for s in range(segments)])  7.68 us
    pallas_call x2, Pallas kernels, run_steps(): pl.pallas_call(functools.partial(steps_kernel, first_step, sections, rows...  6.91 us
    ppermute x6, starting transfers between devices, with_partner(): return lax.ppermute(value, 'segment', [(s, s ^ d) for s in range(segments)])  6.08 us
    ppermute x4, starting transfers between devices, on_swap(): lax.ppermute(value, 'tile', [(i, i ^ 1) for i in range(lax.axis_size('til...  4.73 us
    ppermute x3, waiting for transfers between devices, off_swap(): lax.ppermute(value, 'tile', [p for i in range(1, count - 1, 2) for p in (...  3 us
    squeeze x1, local copies, waits for them, and re-layouts, noise_for(): return lax.dynamic_index_in_dim(augment_noise[0], clip, 0, keepdims=False)  1.3 us
    convert_element_type x1, other arithmetic, per_device(): start = latent_clips[0].astype(f32)  0.98 us
  transfers between devices with their start and end apart: 13, of which 4 were waited for; matrix products, arithmetic and copies ran while one was open for 4% of the time, Pallas kernels for 8%

profile of v1, /device:TPU:1, one launch (start us, length us, event | category | flops | bytes accessed | tf_op | source)
XLA Modules:
  0.0 41.6 jit_solution(13106320553473286873)
XLA Ops:
  0.0 0.0 copy-start
  0.0 0.0 copy-start.1
  0.0 0.0 copy-start.2
  0.0 1.3 %dynamic-slice_bitcast_fusion = (bf16[2,4,128,128]{3,2,1,0:T(8,128)(2,1)S(1)}, bf16[2,4,128,128]{3,2,1,0:T(8,128)(2,1)S(1)}, bf16[2,4,128,128]{3,2,1,0:T(8,128)(2,1)S(1)}, bf16[2,4,128,128]{3,2,1,0:T(8,128)(2,1)S(1)}) fusion(bf16[1,4,2,4,128,128]{5,4,3,2,1,0:T(8,128)(2,1)} %param.6, s32[]{:T(128)S(6)} %select_n.167, s32[]{:T(128)S(6)} %select_n.158, ...), kind=kLoop, calls=%fused_computation.6 | loop fusion | bytes 2097168 | tf_op jit(solution)/shard_map/jit(dynamic_index_in_dim)/squeeze | solution.py:291
  1.3 2.1 %collective-permute-start = (bf16[2,4,128,128]{3,2,1,0:T(8,128)(2,1)S(1)}, bf16[2,4,128,128]{3,2,1,0:T(8,128)(2,1)S(1)}, u32[]{:S(2)}, u32[]{:S(2)}) collective-permute-start(bf16[2,4,128,128]{3,2,1,0:T(8,128)(2,1)S(1)} %get-tuple-element.34), channel_id=1, source_target_pairs={{0,8},{8,0},{16,24},{24,16},{1,9},{9,1},{17,25},{25,17},{2,10},{10... | collective-permute-start | bytes 786440 | tf_op jit(solution)/shard_map/ppermute | solution.py:288
  3.4 1.2 %collective-permute-start.5 = (bf16[2,4,128,128]{3,2,1,0:T(8,128)(2,1)S(1)}, bf16[2,4,128,128]{3,2,1,0:T(8,128)(2,1)S(1)}, u32[]{:S(2)}, u32[]{:S(2)}) collective-permute-start(bf16[2,4,128,128]{3,2,1,0:T(8,128)(2,1)S(1)} %get-tuple-element.33), channel_id=1, source_target_pairs={{0,16},{8,24},{16,0},{24,8},{1,17},{9,25},{17,1},{25,9},{2,18},{10... | collective-permute-start | bytes 786440 | tf_op jit(solution)/shard_map/ppermute | solution.py:288
  4.7 0.0 collective-permute-start.6
  4.7 1.0 %bitcast_convert_fusion = f32[2,4,128,128]{3,2,1,0:T(8,128)S(1)} fusion(bf16[1,2,4,128,128]{4,3,2,1,0:T(8,128)(2,1)} %param.5), kind=kLoop, calls=%fused_computation.2 | loop fusion | flops 131072 | bytes 786432 | tf_op jit(solution)/shard_map/convert_element_type | solution.py:306
  5.7 0.0 copy-done.1
  5.8 0.0 copy-done.2
  5.8 3.7 %collective-permute-done = bf16[2,4,128,128]{3,2,1,0:T(8,128)(2,1)S(1)} collective-permute-done((bf16[2,4,128,128]{3,2,1,0:T(8,128)(2,1)S(1)}, bf16[2,4,128,128]{3,2,1,0:T(8,128)(2,1)S(1)}, u32[]{:S(2)}, u32[]{:S(2)}) %collective-permute-start) | collective-permute-done | bytes 262176 | tf_op jit(solution)/shard_map/ppermute | solution.py:288
  9.5 0.0 copy-done
  9.5 1.2 %collective-permute-start.3 = (bf16[576,128]{1,0:T(8,128)(2,1)S(1)}, bf16[576,128]{1,0:T(8,128)(2,1)S(1)}, u32[]{:S(2)}, u32[]{:S(2)}) collective-permute-start(bf16[576,128]{1,0:T(8,128)(2,1)S(1)} %constant_dynamic-slice_fusion), channel_id=1, source_target_pairs={{0,8},{8,0},{16,24},{24,16},{1,9},{9,1},{17,25},{25,17},{2,10},{10... | collective-permute-start | bytes 442376 | tf_op jit(solution)/shard_map/ppermute | solution.py:288
  10.7 1.2 %collective-permute-start.2 = (bf16[576,128]{1,0:T(8,128)(2,1)S(1)}, bf16[576,128]{1,0:T(8,128)(2,1)S(1)}, u32[]{:S(2)}, u32[]{:S(2)}) collective-permute-start(bf16[576,128]{1,0:T(8,128)(2,1)S(1)} %constant_dynamic-slice_fusion), channel_id=1, source_target_pairs={{0,16},{8,24},{16,0},{24,8},{1,17},{9,25},{17,1},{25,9},{2,18},{10... | collective-permute-start | bytes 442376 | tf_op jit(solution)/shard_map/ppermute | solution.py:288
  11.9 0.3 collective-permute-start.1
  12.2 0.0 collective-permute-done.5
  12.2 3.8 %collective-permute-done.6 = bf16[2,4,128,128]{3,2,1,0:T(8,128)(2,1)S(1)} collective-permute-done((bf16[2,4,128,128]{3,2,1,0:T(8,128)(2,1)S(1)}, bf16[2,4,128,128]{3,2,1,0:T(8,128)(2,1)S(1)}, u32[]{:S(2)}, u32[]{:S(2)}) %collective-permute-start.6) | collective-permute-done | bytes 262176 | tf_op jit(solution)/shard_map/ppermute | solution.py:288
  16.0 0.2 add_convert_fusion.own_ref
  16.3 2.8 %collective-permute-start.7 = (bf16[2,3,128,128]{3,2,1,0:T(8,128)(2,1)S(1)}, bf16[2,3,128,128]{3,2,1,0:T(8,128)(2,1)S(1)}, u32[]{:S(2)}, u32[]{:S(2)}) collective-permute-start(bf16[2,3,128,128]{3,2,1,0:T(8,128)(2,1)S(1)} %get-tuple-element.43), channel_id=1, source_target_pairs={{0,1},{1,0},{2,3},{3,2},{4,5},{5,4},{6,7},{7,6},{8,9},{9,8},{10,11... | collective-permute-start | bytes 589832 | tf_op jit(solution)/shard_map/ppermute | solution.py:271
  19.0 3.1 %collective-permute-start.8 = (bf16[2,3,128,128]{3,2,1,0:T(8,128)(2,1)S(1)}, bf16[2,3,128,128]{3,2,1,0:T(8,128)(2,1)S(1)}, u32[]{:S(2)}, u32[]{:S(2)}) collective-permute-start(bf16[2,3,128,128]{3,2,1,0:T(8,128)(2,1)S(1)} %get-tuple-element.42), channel_id=1, source_target_pairs={{1,2},{2,1},{3,4},{4,3},{5,6},{6,5},{9,10},{10,9},{11,12},{12,11},... | collective-permute-start | bytes 589832 | tf_op jit(solution)/shard_map/ppermute | solution.py:267
  22.2 0.0 collective-permute-done.3
  22.2 0.0 collective-permute-done.2
  22.2 0.2 collective-permute-done.1
  22.4 0.1 pad_maximum_fusion.rest_0_.mine_ref
  22.4 1.8 %collective-permute-start.4 = (bf16[4,576,128]{2,1,0:T(8,128)(2,1)S(1)}, bf16[4,576,128]{2,1,0:T(8,128)(2,1)S(1)}, u32[]{:S(2)}, u32[]{:S(2)}) collective-permute-start(bf16[4,576,128]{2,1,0:T(8,128)(2,1)S(1)} %pad_maximum_fusion.rest_0_.mine_ref), channel_id=1, source_target_pairs={{0,1},{1,0},{2,3},{3,2},{4,5},{5,4},{6,7},{7,6},{8,9},{9,8},{10,11... | collective-permute-start | bytes 1769480 | tf_op jit(solution)/shard_map/ppermute | solution.py:271
  24.3 0.1 select_select_fusion
  24.4 3.1 %collective-permute-start.11 = (bf16[2,3,128,128]{3,2,1,0:T(8,128)(2,1)S(1)}, bf16[2,3,128,128]{3,2,1,0:T(8,128)(2,1)S(1)}, u32[]{:S(2)}, u32[]{:S(2)}) collective-permute-start(bf16[2,3,128,128]{3,2,1,0:T(8,128)(2,1)S(1)} %get-tuple-element.37), channel_id=1, source_target_pairs={{1,2},{2,1},{3,4},{4,3},{5,6},{6,5},{9,10},{10,9},{11,12},{12,11},... | collective-permute-start | bytes 589832 | tf_op jit(solution)/shard_map/ppermute | solution.py:267
  27.6 0.1 collective-permute-start.12
  27.6 0.0 collective-permute-done.7.first_ref
  27.7 0.0 collective-permute-done.8.second_ref
  27.7 0.0 collective-permute-done.4.rest_1_.other_ref
  27.7 2.9 %shard_map.55 = (bf16[2,4,128,128]{3,2,1,0:T(8,128)(2,1)S(1)}, bf16[2,3,128,128]{3,2,1,0:T(8,128)(2,1)S(1)}, bf16[2,3,128,128]{3,2,1,0:T(8,128)(2,1)S(1)}) custom-call(bf16[2,4,128,128]{3,2,1,0:T(8,128)(2,1)S(1)} %add_convert_fusion.own_ref, bf16[2,3,128,128]{3,2,1,0:T(8,128)(2,1)S(1)} %collective-permute-done.7.first_ref, ...), custom_call_target="tpu_custom_call" | custom-call | flops 1358954496 | bytes 524288 | tf_op jit(solution)/shard_map/pallas_call | solution.py:242
  30.6 3.6 %collective-permute-start.9 = (bf16[2,3,128,128]{3,2,1,0:T(8,128)(2,1)S(1)}, bf16[2,3,128,128]{3,2,1,0:T(8,128)(2,1)S(1)}, u32[]{:S(2)}, u32[]{:S(2)}) collective-permute-start(bf16[2,3,128,128]{3,2,1,0:T(8,128)(2,1)S(1)} %get-tuple-element.25), channel_id=1, source_target_pairs={{1,2},{2,1},{3,4},{4,3},{5,6},{6,5},{9,10},{10,9},{11,12},{12,11},... | collective-permute-start | bytes 589832 | tf_op jit(solution)/shard_map/ppermute | solution.py:267
  34.1 0.1 collective-permute-start.10
  34.2 0.3 shard_map.56.rest_0_
  34.5 0.0 collective-permute-done.11.rest_3_
  34.6 0.0 collective-permute-done.12.rest_4_
  34.6 3.0 %collective-permute-done.9.first_ref = bf16[2,3,128,128]{3,2,1,0:T(8,128)(2,1)S(1)} collective-permute-done((bf16[2,3,128,128]{3,2,1,0:T(8,128)(2,1)S(1)}, bf16[2,3,128,128]{3,2,1,0:T(8,128)(2,1)S(1)}, u32[]{:S(2)}, u32[]{:S(2)}) %collective-permute-start.9) | collective-permute-done | bytes 196640 | tf_op jit(solution)/shard_map/ppermute | solution.py:267
  37.6 0.0 collective-permute-done.10.second_ref
  37.6 4.0 %shard_map.57 = bf16[2,4,128,128]{3,2,1,0:T(8,128)(2,1)} custom-call(bf16[2,4,128,128]{3,2,1,0:T(8,128)(2,1)S(1)} %get-tuple-element.24.own_ref, bf16[2,3,128,128]{3,2,1,0:T(8,128)(2,1)S(1)} %collective-permute-done.9.first_ref, bf16[2,3,128,128]{3,2,1,0:T(8,128)(2,1)S(1)} %collective-permute-done.10.second_ref, ...), custom_call_target="tpu_custom_call" | custom-call | flops 1358954496 | bytes 524288 | tf_op jit(solution)/shard_map/pallas_call | solution.py:242
  (8 shorter events, 0.1 us)
Async XLA Ops:
  0.0 9.5 %copy-start = (bf16[1,1152,128]{2,1,0:T(8,128)(2,1)S(1)}, bf16[1,1152,128]{2,1,0:T(8,128)(2,1)}, u32[]{:S(2)}) copy-start(bf16[1,1152,128]{2,1,0:T(8,128)(2,1)} %param.7) | copy-start | bytes 884740
  0.0 5.7 %copy-start.1 = (f32[6,128]{1,0:T(8,128)S(1)}, f32[6,128]{1,0:T(8,128)}, u32[]{:S(2)}) copy-start(f32[6,128]{1,0:T(8,128)} %param.8) | copy-start | bytes 9220
  0.0 5.8 %copy-start.2 = (f32[6,128]{1,0:T(8,128)S(1)}, f32[6,128]{1,0:T(8,128)}, u32[]{:S(2)}) copy-start(f32[6,128]{1,0:T(8,128)} %param.9) | copy-start | bytes 9220
  1.3 8.1 %collective-permute-start = (bf16[2,4,128,128]{3,2,1,0:T(8,128)(2,1)S(1)}, bf16[2,4,128,128]{3,2,1,0:T(8,128)(2,1)S(1)}, u32[]{:S(2)}, u32[]{:S(2)}) collective-permute-start(bf16[2,4,128,128]{3,2,1,0:T(8,128)(2,1)S(1)} %get-tuple-element.34), channel_id=1, source_target_pairs={{0,8},{8,0},{16,24},{24,16},{1,9},{9,1},{17,25},{25,17},{2,10},{10... | collective-permute-start | bytes 786440 | tf_op jit(solution)/shard_map/ppermute | solution.py:288
  3.4 8.8 %collective-permute-start.5 = (bf16[2,4,128,128]{3,2,1,0:T(8,128)(2,1)S(1)}, bf16[2,4,128,128]{3,2,1,0:T(8,128)(2,1)S(1)}, u32[]{:S(2)}, u32[]{:S(2)}) collective-permute-start(bf16[2,4,128,128]{3,2,1,0:T(8,128)(2,1)S(1)} %get-tuple-element.33), channel_id=1, source_target_pairs={{0,16},{8,24},{16,0},{24,8},{1,17},{9,25},{17,1},{25,9},{2,18},{10... | collective-permute-start | bytes 786440 | tf_op jit(solution)/shard_map/ppermute | solution.py:288
  4.7 11.3 %collective-permute-start.6 = (bf16[2,4,128,128]{3,2,1,0:T(8,128)(2,1)S(1)}, bf16[2,4,128,128]{3,2,1,0:T(8,128)(2,1)S(1)}, u32[]{:S(2)}, u32[]{:S(2)}) collective-permute-start(bf16[2,4,128,128]{3,2,1,0:T(8,128)(2,1)S(1)} %get-tuple-element.32), channel_id=1, source_target_pairs={{0,24},{8,16},{16,8},{24,0},{1,25},{9,17},{17,9},{25,1},{2,26},{10... | collective-permute-start | bytes 786440 | tf_op jit(solution)/shard_map/ppermute | solution.py:288
  9.5 12.7 %collective-permute-start.3 = (bf16[576,128]{1,0:T(8,128)(2,1)S(1)}, bf16[576,128]{1,0:T(8,128)(2,1)S(1)}, u32[]{:S(2)}, u32[]{:S(2)}) collective-permute-start(bf16[576,128]{1,0:T(8,128)(2,1)S(1)} %constant_dynamic-slice_fusion), channel_id=1, source_target_pairs={{0,8},{8,0},{16,24},{24,16},{1,9},{9,1},{17,25},{25,17},{2,10},{10... | collective-permute-start | bytes 442376 | tf_op jit(solution)/shard_map/ppermute | solution.py:288
  10.7 11.5 %collective-permute-start.2 = (bf16[576,128]{1,0:T(8,128)(2,1)S(1)}, bf16[576,128]{1,0:T(8,128)(2,1)S(1)}, u32[]{:S(2)}, u32[]{:S(2)}) collective-permute-start(bf16[576,128]{1,0:T(8,128)(2,1)S(1)} %constant_dynamic-slice_fusion), channel_id=1, source_target_pairs={{0,16},{8,24},{16,0},{24,8},{1,17},{9,25},{17,1},{25,9},{2,18},{10... | collective-permute-start | bytes 442376 | tf_op jit(solution)/shard_map/ppermute | solution.py:288
  11.9 10.4 %collective-permute-start.1 = (bf16[576,128]{1,0:T(8,128)(2,1)S(1)}, bf16[576,128]{1,0:T(8,128)(2,1)S(1)}, u32[]{:S(2)}, u32[]{:S(2)}) collective-permute-start(bf16[576,128]{1,0:T(8,128)(2,1)S(1)} %constant_dynamic-slice_fusion), channel_id=1, source_target_pairs={{0,24},{8,16},{16,8},{24,0},{1,25},{9,17},{17,9},{25,1},{2,26},{10... | collective-permute-start | bytes 442376 | tf_op jit(solution)/shard_map/ppermute | solution.py:288
  16.3 11.4 %collective-permute-start.7 = (bf16[2,3,128,128]{3,2,1,0:T(8,128)(2,1)S(1)}, bf16[2,3,128,128]{3,2,1,0:T(8,128)(2,1)S(1)}, u32[]{:S(2)}, u32[]{:S(2)}) collective-permute-start(bf16[2,3,128,128]{3,2,1,0:T(8,128)(2,1)S(1)} %get-tuple-element.43), channel_id=1, source_target_pairs={{0,1},{1,0},{2,3},{3,2},{4,5},{5,4},{6,7},{7,6},{8,9},{9,8},{10,11... | collective-permute-start | bytes 589832 | tf_op jit(solution)/shard_map/ppermute | solution.py:271
  19.0 8.6 %collective-permute-start.8 = (bf16[2,3,128,128]{3,2,1,0:T(8,128)(2,1)S(1)}, bf16[2,3,128,128]{3,2,1,0:T(8,128)(2,1)S(1)}, u32[]{:S(2)}, u32[]{:S(2)}) collective-permute-start(bf16[2,3,128,128]{3,2,1,0:T(8,128)(2,1)S(1)} %get-tuple-element.42), channel_id=1, source_target_pairs={{1,2},{2,1},{3,4},{4,3},{5,6},{6,5},{9,10},{10,9},{11,12},{12,11},... | collective-permute-start | bytes 589832 | tf_op jit(solution)/shard_map/ppermute | solution.py:267
  22.4 5.2 %collective-permute-start.4 = (bf16[4,576,128]{2,1,0:T(8,128)(2,1)S(1)}, bf16[4,576,128]{2,1,0:T(8,128)(2,1)S(1)}, u32[]{:S(2)}, u32[]{:S(2)}) collective-permute-start(bf16[4,576,128]{2,1,0:T(8,128)(2,1)S(1)} %pad_maximum_fusion.rest_0_.mine_ref), channel_id=1, source_target_pairs={{0,1},{1,0},{2,3},{3,2},{4,5},{5,4},{6,7},{7,6},{8,9},{9,8},{10,11... | collective-permute-start | bytes 1769480 | tf_op jit(solution)/shard_map/ppermute | solution.py:271
  24.4 10.1 %collective-permute-start.11 = (bf16[2,3,128,128]{3,2,1,0:T(8,128)(2,1)S(1)}, bf16[2,3,128,128]{3,2,1,0:T(8,128)(2,1)S(1)}, u32[]{:S(2)}, u32[]{:S(2)}) collective-permute-start(bf16[2,3,128,128]{3,2,1,0:T(8,128)(2,1)S(1)} %get-tuple-element.37), channel_id=1, source_target_pairs={{1,2},{2,1},{3,4},{4,3},{5,6},{6,5},{9,10},{10,9},{11,12},{12,11},... | collective-permute-start | bytes 589832 | tf_op jit(solution)/shard_map/ppermute | solution.py:267
  27.6 7.0 %collective-permute-start.12 = (bf16[2,3,128,128]{3,2,1,0:T(8,128)(2,1)S(1)}, bf16[2,3,128,128]{3,2,1,0:T(8,128)(2,1)S(1)}, u32[]{:S(2)}, u32[]{:S(2)}) collective-permute-start(bf16[2,3,128,128]{3,2,1,0:T(8,128)(2,1)S(1)} %get-tuple-element.36), channel_id=1, source_target_pairs={{0,1},{1,0},{2,3},{3,2},{4,5},{5,4},{6,7},{7,6},{8,9},{9,8},{10,11... | collective-permute-start | bytes 589832 | tf_op jit(solution)/shard_map/ppermute | solution.py:271
  30.6 7.0 %collective-permute-start.9 = (bf16[2,3,128,128]{3,2,1,0:T(8,128)(2,1)S(1)}, bf16[2,3,128,128]{3,2,1,0:T(8,128)(2,1)S(1)}, u32[]{:S(2)}, u32[]{:S(2)}) collective-permute-start(bf16[2,3,128,128]{3,2,1,0:T(8,128)(2,1)S(1)} %get-tuple-element.25), channel_id=1, source_target_pairs={{1,2},{2,1},{3,4},{4,3},{5,6},{6,5},{9,10},{10,9},{11,12},{12,11},... | collective-permute-start | bytes 589832 | tf_op jit(solution)/shard_map/ppermute | solution.py:267
  34.1 3.4 %collective-permute-start.10 = (bf16[2,3,128,128]{3,2,1,0:T(8,128)(2,1)S(1)}, bf16[2,3,128,128]{3,2,1,0:T(8,128)(2,1)S(1)}, u32[]{:S(2)}, u32[]{:S(2)}) collective-permute-start(bf16[2,3,128,128]{3,2,1,0:T(8,128)(2,1)S(1)} %get-tuple-element.26), channel_id=1, source_target_pairs={{0,1},{1,0},{2,3},{3,2},{4,5},{5,4},{6,7},{7,6},{8,9},{9,8},{10,11... | collective-permute-start | bytes 589832 | tf_op jit(solution)/shard_map/ppermute | solution.py:271
